TPU v7x, 128 devices: a whole 4x4x4 slice. The times are simulated.
128 devices in a mesh: var: 8 (over z, x_hi), patch: 8 (over y, core), win: 2 (over x_lo).
Axes of the slice: x: 4 (x_hi: 2, x_lo: 2; x = x_hi * 2 + x_lo), y: 4, z: 4, core: 2. Of those that a mesh axis runs over, the one named last changes fastest.
Arguments:
- fields: bfloat16 [480, 16, 1024], P(('win', 'var'), 'patch'), parts along dimension 0, may hold values from -6 to 6
- var_ids: int32 [240], replicated, may hold values from 0 to 239, each once
- level_of: int32 [240], replicated, may hold values from 0 to 37
- window_offset: int32 [2], P('win'), parts along dimension 0, may hold values from 0 to 164
- w_embed: bfloat16 [240, 16, 512], replicated, may hold values from -1.5 to 1.5
- var_emb: bfloat16 [240, 512], replicated, may hold values from -6 to 6
- w_key: bfloat16 [512, 512], replicated, may hold values from -0.25 to 0.25
- w_value: bfloat16 [512, 512], replicated, may hold values from -0.25 to 0.25
- w_out: bfloat16 [512, 512], replicated, may hold values from -0.25 to 0.25
- latent_query: float32 [8, 64], replicated, may hold values from -9 to 9
- bias_table: float32 [38, 8], replicated, may hold values from -4 to 300
- lat_emb: bfloat16 [180, 512], replicated, may hold values from -3 to 3
- d_aggregated: bfloat16 [32, 64, 512], P('win', ('var', 'patch')), parts along dimension 0, may hold values from -6 to 6
Outputs:
- aggregated: bfloat16 [32, 64, 512], P('win', ('var', 'patch')), parts along dimension 0
- embed_grad_rows: float32 [480, 16, 512], P(('win', 'var')), parts along dimension 0
- var_grad_rows: float32 [480, 512], P(('win', 'var')), parts along dimension 0
- key_grad: float32 [1024, 512], P('win'), parts along dimension 0
- value_grad: float32 [1024, 512], P('win'), parts along dimension 0
There are 2 independent parts, one for each index of `win`. A program takes and returns all parts, laid end to end along the dimension named above; an argument that names none is the same for every part. Nothing has to cross between parts.
All inputs are finite; a program needn't handle non-finite values.
Results may differ from a plain program's by a relative error of at most 0.017.
Values may be sent and summed in bfloat16 or wider, within the bound.
A program may use at most 128 MiB of HBM per device.

v0:
```python
import jax
import jax.numpy as jnp
from jax import lax
from jax.sharding import PartitionSpec as P


def attend(tokens, bias_rows, latent_query, w_key, w_value, w_out, lat_rows, cotangent):
    var_count, patch_count, width = tokens.shape
    head_count, head_size = latent_query.shape
    score_scale = head_size ** (-0.5)
    flat_tokens = tokens.reshape(var_count * patch_count, width)
    key_rows = jnp.dot(flat_tokens, w_key, preferred_element_type=jnp.float32)
    key_heads = key_rows.reshape(var_count, patch_count, head_count, head_size)
    inverse_rms = lax.rsqrt(jnp.mean(key_heads * key_heads, axis=-1, keepdims=True) + 1e-06)
    normed = key_heads * inverse_rms
    scores = (
        jnp.einsum("vphe,he->phv", normed, latent_query, precision=lax.Precision.HIGHEST)
        * score_scale
        + bias_rows.T[None]
    )
    largest = jnp.max(scores, axis=-1, keepdims=True)
    raised = jnp.exp(scores - largest)
    weights = raised / jnp.sum(raised, axis=-1, keepdims=True)
    attn_rounded = weights.astype(jnp.bfloat16)
    mixed_rows = jnp.einsum(
        "phv,vpd->phd", attn_rounded, tokens, preferred_element_type=jnp.float32
    ).astype(jnp.bfloat16)
    value_heads = w_value.reshape(width, head_count, head_size)
    context = (
        jnp.einsum("phd,dhe->phe", mixed_rows, value_heads, preferred_element_type=jnp.float32)
        .astype(jnp.bfloat16)
        .reshape(patch_count, width)
    )
    output = (jnp.dot(context, w_out, preferred_element_type=jnp.float32) + lat_rows).astype(
        jnp.bfloat16
    )
    grad_context = jnp.dot(cotangent, w_out.T, preferred_element_type=jnp.float32).astype(
        jnp.bfloat16
    )
    grad_heads = grad_context.reshape(patch_count, head_count, head_size)
    value_grad = jnp.einsum(
        "phd,phe->dhe", mixed_rows, grad_heads, preferred_element_type=jnp.float32
    ).reshape(width, width)
    grad_mixed = jnp.einsum(
        "phe,dhe->phd", grad_heads, value_heads, preferred_element_type=jnp.float32
    ).astype(jnp.bfloat16)
    grad_attn = jnp.einsum("phd,vpd->phv", grad_mixed, tokens, preferred_element_type=jnp.float32)
    grad_scores = weights * (grad_attn - jnp.sum(weights * grad_attn, axis=-1, keepdims=True))
    grad_normed = (
        jnp.einsum("phv,he->vphe", grad_scores, latent_query, precision=lax.Precision.HIGHEST)
        * score_scale
    )
    grad_keys = (
        inverse_rms
        * (grad_normed - normed * jnp.mean(grad_normed * normed, axis=-1, keepdims=True))
    ).astype(jnp.bfloat16)
    grad_keys = grad_keys.reshape(var_count * patch_count, width)
    key_grad = jnp.einsum("nd,ne->de", flat_tokens, grad_keys, preferred_element_type=jnp.float32)
    through_keys = jnp.dot(grad_keys, w_key.T, preferred_element_type=jnp.float32).reshape(
        var_count, patch_count, width
    )
    through_values = jnp.einsum(
        "phv,phd->vpd", attn_rounded, grad_mixed, preferred_element_type=jnp.float32
    )
    token_grad = (through_values + through_keys).astype(jnp.bfloat16)
    return (output, token_grad, key_grad, value_grad)


def embed_tokens(patches, w_rows, emb_rows):
    summed = jnp.einsum("vpk,vkd->vpd", patches, w_rows, preferred_element_type=jnp.float32)
    return (summed + emb_rows[:, None, :]).astype(jnp.bfloat16)


def local(
    fields,
    var_ids,
    level_of,
    window_offset,
    w_embed,
    var_emb,
    w_key,
    w_value,
    w_out,
    latent_query,
    bias_table,
    lat_emb,
    d_aggregated,
):
    local_vars, local_rows, merged = fields.shape
    pixels = w_embed.shape[1]
    width = w_embed.shape[2]
    row_count = d_aggregated.shape[0]
    own_cols = d_aggregated.shape[1]
    level_count = bias_table.shape[0]
    all_cols = merged // pixels
    var_devices = lax.axis_size("var")
    patch_devices = lax.axis_size("patch")
    levels = jnp.take(level_of, var_ids, axis=0)
    one_hot = (levels[:, None] == jnp.arange(level_count, dtype=jnp.int32)[None, :]).astype(
        jnp.float32
    )
    bias_rows = jnp.dot(one_hot, bias_table, precision=lax.Precision.HIGHEST)
    lat_slice = lax.dynamic_slice_in_dim(lat_emb, window_offset[0], row_count, 0)
    lat_rows = lat_slice[:, None, :].reshape(row_count * own_cols, width)
    cotangent = d_aggregated.reshape(row_count * own_cols, width)
    row_start = lax.axis_index("var") * local_vars
    local_ids = lax.dynamic_slice_in_dim(var_ids, row_start, local_vars, 0)
    w_rows = jnp.take(w_embed, local_ids, axis=0)
    emb_rows = jnp.take(var_emb, local_ids, axis=0)
    patches = fields.reshape(local_vars, local_rows * all_cols, pixels)
    local_tokens = embed_tokens(patches, w_rows, emb_rows).reshape(
        local_vars, local_rows, all_cols * width
    )
    owned_tokens = lax.all_to_all(
        lax.all_to_all(local_tokens, "var", split_axis=2, concat_axis=0, tiled=True),
        "patch",
        split_axis=2,
        concat_axis=1,
        tiled=True,
    )
    output, token_grad, key_grad, value_grad = attend(
        owned_tokens, bias_rows, latent_query, w_key, w_value, w_out, lat_rows, cotangent
    )
    returned = lax.all_to_all(
        lax.all_to_all(token_grad, "var", split_axis=0, concat_axis=2, tiled=True),
        "patch",
        split_axis=1,
        concat_axis=2,
        tiled=True,
    )
    returned = returned.reshape(
        local_vars, local_rows, patch_devices, var_devices, own_cols * width
    )
    local_grad = returned.transpose(0, 1, 3, 2, 4).reshape(local_vars, local_rows * all_cols, width)
    embed_part = jnp.einsum("vpk,vpd->vkd", patches, local_grad, preferred_element_type=jnp.float32)
    var_part = jnp.sum(local_grad, axis=1, dtype=jnp.float32)
    embed_grad, var_grad = (
        lax.psum(embed_part.astype(jnp.bfloat16), "patch").astype(jnp.float32),
        lax.psum(var_part.astype(jnp.bfloat16), "patch").astype(jnp.float32),
    )
    key_grad, value_grad = lax.psum((key_grad, value_grad), ("var", "patch"))
    return (output.reshape(row_count, own_cols, width), embed_grad, var_grad, key_grad, value_grad)


def solution(mesh):
    in_specs = (
        P(("win", "var"), "patch", None),
        P(),
        P(),
        P("win"),
        P(),
        P(),
        P(),
        P(),
        P(),
        P(),
        P(),
        P(),
        P("win", ("var", "patch"), None),
    )
    out_specs = (
        P("win", ("var", "patch"), None),
        P(("win", "var"), None, None),
        P(("win", "var"), None),
        P("win", None),
        P("win", None),
    )
    return jax.shard_map(local, mesh=mesh, in_specs=in_specs, out_specs=out_specs, check_vma=False)
```

profile of v0, /device:TPU:1, one launch (start us, length us, event | category | flops | bytes accessed | tf_op | source)
XLA Modules:
  0.0 1303.5 jit_solution(16177951120995973303)
XLA Ops:
  14.2 5.0 fusion.8
  19.2 6.3 copy.93
  25.4 9.9 reshape.98
  35.4 38.3 %copy.94 = bf16[30,2,32768]{0,1,2:T(2,128)(2,1)} copy(bf16[30,2,32768]{2,1,0:T(2,128)(2,1)} %reshape.98) | data formatting | bytes 7864320 | tf_op jit(solution)/shard_map/reshape | solution.py:111
  73.7 39.7 %reshape.143 = bf16[8,2,122880]{2,1,0:T(2,128)(2,1)} reshape(bf16[32768,2,30]{2,1,0:T(2,128)(2,1)} %bitcast.123) | data formatting | bytes 7864320
  113.4 56.1 %all_to_all.66 = bf16[8,2,122880]{2,1,0:T(2,128)(2,1)} all-to-all(bf16[8,2,122880]{2,1,0:T(2,128)(2,1)} %reshape.143), channel_id=1, replica_groups=mesh['var'=8,'patch'=8,'win'=2] {'var'}, dimensions={0} | all-to-all | bytes 7864320 | tf_op jit(solution)/shard_map/all_to_all | solution.py:115
  169.5 46.5 %reshape.144 = bf16[32768,2,30]{2,1,0:T(2,128)(2,1)} reshape(bf16[8,2,122880]{2,1,0:T(2,128)(2,1)} %all_to_all.66) | data formatting | bytes 7864320
  216.0 40.5 %copy.95 = bf16[30,2,8,4096]{3,1,0,2:T(2,128)(2,1)} copy(bf16[30,2,8,4096]{0,1,3,2:T(2,128)(2,1)} %bitcast.124) | data formatting | bytes 7864320 | tf_op jit(solution)/shard_map/all_to_all | solution.py:115
  256.6 14.9 %copy.96 = bf16[240,2,4096]{0,1,2:T(2,128)(2,1)} copy(bf16[240,2,4096]{2,1,0:T(2,128)(2,1)} %bitcast.132) | data formatting | bytes 7864320 | tf_op jit(solution)/shard_map/all_to_all | solution.py:115
  271.5 6.5 all-to-all-start.1
  281.3 45.5 %all-to-all-done.1 = bf16[240,2,4096]{0,1,2:T(2,128)(2,1)} async-done(((bf16[240,2,4096]{0,1,2:T(2,128)(2,1)}), bf16[240,2,4096]{0,1,2:T(2,128)(2,1)}, u32[]{:S(2)}, u32[]{:S(2)}) %all-to-all-start.1) | async-done | bytes 3932192 | tf_op jit(solution)/shard_map/all_to_all | solution.py:114
  326.9 15.9 %copy.97 = bf16[240,2,8,512]{3,1,2,0:T(2,128)(2,1)} copy(bf16[240,2,8,512]{0,1,3,2:T(2,128)(2,1)} %bitcast.5) | data formatting | bytes 7864320 | tf_op jit(solution)/shard_map/all_to_all | solution.py:114
  342.7 9.1 reshape.136
  351.8 9.8 multiply_reduce_fusion
  361.8 11.1 copy.128
  372.8 6.8 broadcast_multiply_fusion
  379.6 33.2 %fusion.5 = f32[8,1,240,16]{2,1,3,0:T(1,128)S(1)} fusion(f32[8,64,1,1]{1,2,3,0:T(1,128)S(1)} %bitcast.140, f32[240,16,8,64]{3,1,2,0:T(8,128)S(1)} %broadcast_multiply_fusion), kind=kOutput, calls=%fused_computation.10 | convolution fusion | flops 23592960 | bytes 7989248 | tf_op jit(solution)/shard_map/vphe,he->phv/dot_general | solution.py:17
  416.8 15.7 %fusion.2 = f32[240,16,8]{1,2,0:T(8,128)S(1)} fusion(f32[8,64]{1,0:T(8,128)S(1)} %copy-done.15, f32[8,16,240]{1,0,2:T(8,128)S(1)} %copy.107, f32[240,16,8,64]{3,1,2,0:T(8,128)} %get-tuple-element.10, f32[240,16,8]{1,2,0:T(8,128)S(1)} %add_rsqrt_fusion), kind=kLoop, calls=%fused_computation.7 | loop fusion | flops 9799680 | bytes 8235008 | tf_op jit(solution)/shard_map/reduce_sum | solution.py:55
  432.5 17.5 %fusion.4 = bf16[240,16,8,64]{3,1,2,0:T(8,128)(2,1)} fusion(f32[240,16,8]{1,2,0:T(8,128)S(1)} %broadcast_multiply_fusion.1, f32[8,64]{1,0:T(8,128)S(1)} %copy-done.15, f32[8,16,240]{1,0,2:T(8,128)S(1)} %copy.107, f32[240,16,8]{1,2,0:T(8,128)S(1)} %add_rsqrt_fusion, f32[240,16,8,64]{3,1,2,0:T(8,128)} %get-tuple-element.10), kind=kLoop, calls=%fused_computation.9 | loop fusion | flops 13762560 | bytes 12167168 | tf_op jit(solution)/shard_map/convert_element_type | solution.py:56
  450.0 10.4 copy.108
  460.4 4.7 fusion.21
  468.7 49.6 %all_to_all.67 = bf16[240,16,512]{2,1,0:T(8,128)(2,1)S(1)} all-to-all(bf16[240,16,512]{2,1,0:T(8,128)(2,1)S(1)} %copy.111), channel_id=1, replica_groups=mesh['var'=8,'patch'=8,'win'=2] {'var'}, dimensions={0} | all-to-all | bytes 7864320 | tf_op jit(solution)/shard_map/all_to_all | solution.py:125
  522.5 6.4 reshape.142
  528.9 6.4 all-to-all-start.3
  535.5 10.3 copy.117
  545.8 9.1 reshape.106
  554.9 11.2 reshape.107
  569.4 5.3 fusion.47
  574.7 9.5 all-to-all-done.3
  601.4 21.2 %psum.29 = bf16[30,512]{1,0:T(8,128)(2,1)S(1)} all-reduce(bf16[30,512]{1,0:T(8,128)(2,1)S(1)} %bitcast_reduce_fusion.1), channel_id=1, replica_groups=mesh['var'=8,'patch'=8,'win'=2] {'patch'}, use_global_device_ids=true, to_apply=%region_7.8 | all-reduce | flops 15360 | bytes 61440 | tf_op jit(solution)/shard_map/psum | solution.py:139
  623.2 23.5 %all-reduce.4.cloned.1.call-done = bf16[30,16,512]{2,1,0:T(8,128)(2,1)} async-done(((bf16[30,16,512]{2,1,0:T(8,128)(2,1)}), bf16[30,16,512]{2,1,0:T(8,128)(2,1)}) %all-reduce.4.cloned.1.call-update) | async-done | bytes 491536 | tf_op jit(solution)/shard_map/psum | solution.py:138
  648.7 643.1 %all-reduce.6.cloned.1.call-done = (f32[512,512]{1,0:T(8,128)}, f32[512,512]{1,0:T(8,128)}) async-done(((f32[512,512]{1,0:T(8,128)}, f32[512,512]{1,0:T(8,128)}), (f32[512,512]{1,0:T(8,128)}, f32[512,512]{1,0:T(8,128)})) %all-reduce.6.cloned.1.call-update) | async-done | bytes 2097168 | tf_op jit(solution)/shard_map/psum | solution.py:141
  (83 shorter events, 49.3 us)
Async XLA Ops:
  7.2 271.2 %copy-start = (bf16[512,512]{1,0:T(8,128)(2,1)S(1)}, bf16[512,512]{1,0:T(8,128)(2,1)}, u32[]{:S(2)}) copy-start(bf16[512,512]{1,0:T(8,128)(2,1)} %param.21) | copy-start | bytes 1572868
  14.1 11.4 copy-start.10
  271.4 6.5 copy-start.5
  271.4 6.7 copy-start.12
  271.4 7.0 copy-start.16
  271.4 7.3 copy-start.17
  271.5 7.4 copy-start.1
  271.5 9.3 copy-start.18
  271.5 55.4 %all-to-all-start.1 = ((bf16[240,2,4096]{0,1,2:T(2,128)(2,1)}), bf16[240,2,4096]{0,1,2:T(2,128)(2,1)}, u32[]{:S(2)}, u32[]{:S(2)}) async-start(bf16[240,2,4096]{0,1,2:T(2,128)(2,1)} %copy.96), calls=%async_computation.1 | async-start | bytes 8388608 | tf_op jit(solution)/shard_map/all_to_all | solution.py:114
  278.8 64.0 %copy-start.13 = (bf16[16,8,64]{2,1,0:T(8,128)(2,1)}, bf16[16,8,64]{2,1,0:T(8,128)(2,1)S(1)}, u32[]{:S(2)}) copy-start(bf16[16,8,64]{2,1,0:T(8,128)(2,1)S(1)} %reshape.103) | copy-start | bytes 49156
  281.3 131.8 %copy-start.8 = (bf16[16,8,512]{2,0,1:T(8,128)(2,1)}, bf16[16,8,512]{2,0,1:T(8,128)(2,1)S(1)}, u32[]{:S(2)}) copy-start(bf16[16,8,512]{2,0,1:T(8,128)(2,1)S(1)} %fusion.13) | copy-start | bytes 393220
  372.8 6.8 copy-start.15
  379.6 33.5 %copy-start.2 = (bf16[240,8,2,512]{3,0,2,1:T(8,128)(2,1)S(1)}, bf16[240,8,2,512]{3,0,2,1:T(8,128)(2,1)}, u32[]{:S(2)}) copy-start(bf16[240,8,2,512]{3,0,2,1:T(8,128)(2,1)} %copy.128) | copy-start | bytes 11796484
  413.1 1.1 copy-start.6
  460.4 4.7 copy-start.7
  460.4 4.7 copy-start.9
  528.9 55.3 %all-to-all-start.3 = ((bf16[30,16,4096]{2,0,1:T(8,128)(2,1)}), bf16[30,16,4096]{2,0,1:T(8,128)(2,1)}, u32[]{:S(2)}, u32[]{:S(2)}) async-start(bf16[30,16,4096]{2,0,1:T(8,128)(2,1)} %reshape.142), calls=%async_computation.3 | async-start | bytes 8388608 | tf_op jit(solution)/shard_map/all_to_all | solution.py:124
  535.3 111.3 %all-reduce.4.cloned.1.call-start = ((), (), s32[]{:S(2)}) async-start(), calls=%async_computation.4 | async-start | bytes 983040 | tf_op jit(solution)/shard_map/psum | solution.py:138
  566.1 3.3 copy-start.4
  574.7 15.8 %copy-start.11 = (bf16[30,128,16]{1,2,0:T(8,128)(2,1)S(1)}, bf16[30,128,16]{1,2,0:T(8,128)(2,1)}, u32[]{:S(2)}) copy-start(bf16[30,128,16]{1,2,0:T(8,128)(2,1)} %copy-done.10) | copy-start | bytes 368644
  588.5 1.9 copy-start.3
  588.6 3.6 copy-start.14
  591.9 700.0 %all-reduce.6.cloned.1.call-start = ((), (), s32[]{:S(2)}) async-start(), calls=%async_computation.5 | async-start | bytes 4194304 | tf_op jit(solution)/shard_map/psum | solution.py:141
Sparse Core Ops, SparseCore 0:
  592.0 54.5 all-reduce.3
  649.8 641.9 all-reduce.5
where the time goes:
time: 1320 us; the launch traced here: 1300 us
  waiting for transfers between devices  722 us (55%)
  local copies, waits for them, and re-layouts  313 us (24%)
  blocking collectives  127 us (10%)
  matrix products  67.6 us (5%)
  other arithmetic  46 us (3%)
  between operations  15.3 us (1%)
  starting transfers between devices  13.4 us (1%)
    psum x1, waiting for transfers between devices, local(): key_grad, value_grad = lax.psum((key_grad, value_grad), ('var', 'patch'))  643 us
    unnamed x46, local copies, waits for them, and re-layouts  98.9 us
    all_to_all x1, blocking collectives, local(): lax.all_to_all(local_tokens, 'var', split_axis=2, concat_axis=0, tiled=True)  56.1 us
    all_to_all x2, local copies, waits for them, and re-layouts, local(): lax.all_to_all(local_tokens, 'var', split_axis=2, concat_axis=0, tiled=True)  55.4 us
    all_to_all x1, blocking collectives, local(): lax.all_to_all(token_grad, 'var', split_axis=0, concat_axis=2, tiled=True)  49.6 us
    reshape x2, local copies, waits for them, and re-layouts, local(): embed_tokens(patches, w_rows, emb_rows)  48.2 us
    all_to_all x1, waiting for transfers between devices, local(): lax.all_to_all(lax.all_to_all(local_tokens, 'var', split_axis=2, concat_a...  45.5 us
    dot_general x1, matrix products, attend(): jnp.einsum('vphe,he->phv', normed, latent_query, precision=lax.Precision....  33.2 us
  transfers between devices with their start and end apart: 4, of which 4 were waited for; matrix products, arithmetic and copies ran while one was open for 4% of the time, Pallas kernels for 0%

commit v1 on v0

--- a/solution.py
+++ b/solution.py
@@ -138,7 +138,7 @@
         lax.psum(embed_part.astype(jnp.bfloat16), "patch").astype(jnp.float32),
         lax.psum(var_part.astype(jnp.bfloat16), "patch").astype(jnp.float32),
     )
-    key_grad, value_grad = lax.psum((key_grad, value_grad), ("var", "patch"))
+    key_grad, value_grad = lax.psum(lax.psum((key_grad, value_grad), "var"), "patch")
     return (output.reshape(row_count, own_cols, width), embed_grad, var_grad, key_grad, value_grad)
 
 

time: 1320 us -> 836 us (0.63)
  waiting for transfers between devices: 722 us -> 238 us
    psum x1 -> x2, waiting for transfers between devices: 643 us -> 156 us  [the longest x1 90.4 us: local(): lax.psum((key_grad, value_grad), 'var')]
    unnamed x46 -> x44, local copies, waits for them, and re-layouts: 98.9 us -> 98.5 us
  transfers between devices with their start and end apart: 4 -> 5, of which waited for: 4 -> 5; matrix products, arithmetic and copies ran while one was open for 4% -> 7% of each run, Pallas kernels for 0% -> 0%
where the time goes in v1:
time: 836 us; the launch traced here: 822 us
  local copies, waits for them, and re-layouts  312 us (37%)
  waiting for transfers between devices  238 us (28%)
  blocking collectives  128 us (15%)
  matrix products  68.8 us (8%)
  other arithmetic  46 us (6%)
  between operations  15 us (2%)
  starting transfers between devices  13.4 us (2%)
    unnamed x44, local copies, waits for them, and re-layouts  98.5 us
    psum x1, waiting for transfers between devices, local(): lax.psum((key_grad, value_grad), 'var')  90.4 us
    psum x1, waiting for transfers between devices, local(): lax.psum(lax.psum((key_grad, value_grad), 'var'), 'patch')  65.8 us
    all_to_all x1, blocking collectives, local(): lax.all_to_all(local_tokens, 'var', split_axis=2, concat_axis=0, tiled=True)  56.1 us
    all_to_all x2, local copies, waits for them, and re-layouts, local(): lax.all_to_all(local_tokens, 'var', split_axis=2, concat_axis=0, tiled=True)  55.4 us
    all_to_all x1, blocking collectives, local(): lax.all_to_all(token_grad, 'var', split_axis=0, concat_axis=2, tiled=True)  49.6 us
    reshape x2, local copies, waits for them, and re-layouts, local(): embed_tokens(patches, w_rows, emb_rows)  48.4 us
    all_to_all x1, waiting for transfers between devices, local(): lax.all_to_all(lax.all_to_all(local_tokens, 'var', split_axis=2, concat_a...  45.5 us
  transfers between devices with their start and end apart: 5, of which 5 were waited for; matrix products, arithmetic and copies ran while one was open for 7% of the time, Pallas kernels for 0%

profile of v1, /device:TPU:1, one launch (start us, length us, event | category | flops | bytes accessed | tf_op | source)
XLA Modules:
  0.0 821.7 jit_solution(7448198468845450934)
XLA Ops:
  14.2 5.0 fusion.8
  19.2 6.3 copy.93
  25.5 9.9 %reshape.98 = bf16[30,2,32768]{2,1,0:T(2,128)(2,1)} reshape(bf16[30,128,512]{2,1,0:T(8,128)(2,1)} %copy.93) | data formatting | bytes 7864320 | tf_op jit(solution)/shard_map/reshape | solution.py:111
  35.4 38.4 %copy.94 = bf16[30,2,32768]{0,1,2:T(2,128)(2,1)} copy(bf16[30,2,32768]{2,1,0:T(2,128)(2,1)} %reshape.98) | data formatting | bytes 7864320 | tf_op jit(solution)/shard_map/reshape | solution.py:111
  73.8 39.8 %reshape.143 = bf16[8,2,122880]{2,1,0:T(2,128)(2,1)} reshape(bf16[32768,2,30]{2,1,0:T(2,128)(2,1)} %bitcast.123) | data formatting | bytes 7864320
  113.6 56.1 %all_to_all.66 = bf16[8,2,122880]{2,1,0:T(2,128)(2,1)} all-to-all(bf16[8,2,122880]{2,1,0:T(2,128)(2,1)} %reshape.143), channel_id=1, replica_groups=mesh['var'=8,'patch'=8,'win'=2] {'var'}, dimensions={0} | all-to-all | bytes 7864320 | tf_op jit(solution)/shard_map/all_to_all | solution.py:115
  169.7 46.5 %reshape.144 = bf16[32768,2,30]{2,1,0:T(2,128)(2,1)} reshape(bf16[8,2,122880]{2,1,0:T(2,128)(2,1)} %all_to_all.66) | data formatting | bytes 7864320
  216.2 40.5 %copy.95 = bf16[30,2,8,4096]{3,1,0,2:T(2,128)(2,1)} copy(bf16[30,2,8,4096]{0,1,3,2:T(2,128)(2,1)} %bitcast.124) | data formatting | bytes 7864320 | tf_op jit(solution)/shard_map/all_to_all | solution.py:115
  256.7 14.9 %copy.96 = bf16[240,2,4096]{0,1,2:T(2,128)(2,1)} copy(bf16[240,2,4096]{2,1,0:T(2,128)(2,1)} %bitcast.132) | data formatting | bytes 7864320 | tf_op jit(solution)/shard_map/all_to_all | solution.py:115
  271.6 6.5 all-to-all-start.1
  281.5 45.5 %all-to-all-done.1 = bf16[240,2,4096]{0,1,2:T(2,128)(2,1)} async-done(((bf16[240,2,4096]{0,1,2:T(2,128)(2,1)}), bf16[240,2,4096]{0,1,2:T(2,128)(2,1)}, u32[]{:S(2)}, u32[]{:S(2)}) %all-to-all-start.1) | async-done | bytes 3932192 | tf_op jit(solution)/shard_map/all_to_all | solution.py:114
  327.0 15.8 %copy.97 = bf16[240,2,8,512]{3,1,2,0:T(2,128)(2,1)} copy(bf16[240,2,8,512]{0,1,3,2:T(2,128)(2,1)} %bitcast.5) | data formatting | bytes 7864320 | tf_op jit(solution)/shard_map/all_to_all | solution.py:114
  342.9 9.1 %reshape.136 = bf16[240,16,512,1]{2,1,0,3:T(8,128)(2,1)} reshape(bf16[240,8,2,512]{3,2,1,0:T(2,128)(2,1)} %bitcast.125) | data formatting | bytes 7864320 | tf_op jit(solution)/shard_map/dot_general | solution.py:12
  352.0 9.8 %multiply_reduce_fusion = (f32[240,16,8]{1,2,0:T(8,128)S(1)}, f32[240,16,8,64]{3,1,2,0:T(8,128)}) fusion(bf16[8,64,512,1]{2,1,0,3:T(8,128)(2,1)S(1)} %bitcast.139, bf16[240,16,512,1]{2,1,0,3:T(8,128)(2,1)} %reshape.136), kind=kOutput, calls=%fused_computation.13 | convolution fusion | flops 2017167360 | bytes 12443648 | tf_op jit(solution)/shard_map/dot_general | solution.py:12
  361.9 11.1 %copy.128 = bf16[240,8,2,512]{3,0,2,1:T(8,128)(2,1)} copy(bf16[240,8,2,512]{0,2,3,1:T(2,128)(2,1)} %bitcast.41) | data formatting | bytes 7864320 | tf_op jit(solution)/shard_map/dot_general | solution.py:12
  373.0 6.8 broadcast_multiply_fusion
  379.8 33.2 %fusion.5 = f32[8,1,240,16]{2,1,3,0:T(1,128)S(1)} fusion(f32[8,64,1,1]{1,2,3,0:T(1,128)S(1)} %bitcast.140, f32[240,16,8,64]{3,1,2,0:T(8,128)S(1)} %broadcast_multiply_fusion), kind=kOutput, calls=%fused_computation.10 | convolution fusion | flops 23592960 | bytes 7989248 | tf_op jit(solution)/shard_map/vphe,he->phv/dot_general | solution.py:17
  416.9 15.7 %fusion.2 = f32[240,16,8]{1,2,0:T(8,128)S(1)} fusion(f32[8,64]{1,0:T(8,128)S(1)} %copy-done.14, f32[8,16,240]{1,0,2:T(8,128)S(1)} %copy.107, f32[240,16,8,64]{3,1,2,0:T(8,128)} %get-tuple-element.12, f32[240,16,8]{1,2,0:T(8,128)S(1)} %add_rsqrt_fusion), kind=kLoop, calls=%fused_computation.7 | loop fusion | flops 9799680 | bytes 8235008 | tf_op jit(solution)/shard_map/reduce_sum | solution.py:55
  432.7 17.5 %fusion.4 = bf16[240,16,8,64]{3,1,2,0:T(8,128)(2,1)} fusion(f32[240,16,8]{1,2,0:T(8,128)S(1)} %broadcast_multiply_fusion.1, f32[8,64]{1,0:T(8,128)S(1)} %copy-done.14, f32[8,16,240]{1,0,2:T(8,128)S(1)} %copy.107, f32[240,16,8]{1,2,0:T(8,128)S(1)} %add_rsqrt_fusion, f32[240,16,8,64]{3,1,2,0:T(8,128)} %get-tuple-element.12), kind=kLoop, calls=%fused_computation.9 | loop fusion | flops 13762560 | bytes 12167168 | tf_op jit(solution)/shard_map/convert_element_type | solution.py:56
  450.2 10.4 %copy.108 = bf16[240,16,8,64]{0,3,2,1:T(8,128)(2,1)} copy(bf16[240,16,8,64]{3,1,2,0:T(8,128)(2,1)} %fusion.4) | data formatting | bytes 7864320 | tf_op jit(solution)/shard_map/convert_element_type | solution.py:56
  468.9 49.6 %all_to_all.67 = bf16[240,16,512]{2,1,0:T(8,128)(2,1)S(1)} all-to-all(bf16[240,16,512]{2,1,0:T(8,128)(2,1)S(1)} %copy.111), channel_id=1, replica_groups=mesh['var'=8,'patch'=8,'win'=2] {'var'}, dimensions={0} | all-to-all | bytes 7864320 | tf_op jit(solution)/shard_map/all_to_all | solution.py:125
  522.7 6.4 reshape.142
  529.1 6.4 all-to-all-start.3
  535.7 10.3 %copy.117 = bf16[240,16,8,64]{3,2,1,0:T(8,128)(2,1)} copy(bf16[240,16,8,64]{3,1,2,0:T(8,128)(2,1)} %fusion.4) | data formatting | bytes 7864320 | tf_op jit(solution)/shard_map/convert_element_type | solution.py:56
  546.0 9.1 %reshape.106 = bf16[3840,512]{1,0:T(8,128)(2,1)} reshape(bf16[240,8,2,512]{3,2,1,0:T(2,128)(2,1)} %bitcast.126) | data formatting | bytes 7864320 | tf_op jit(solution)/shard_map/reshape | solution.py:11
  555.0 11.2 %reshape.107 = bf16[3840,512]{1,0:T(8,128)(2,1)} reshape(bf16[240,16,8,64]{3,2,1,0:T(8,128)(2,1)} %copy.117) | data formatting | bytes 7864320 | tf_op jit(solution)/shard_map/reshape | solution.py:57
  570.7 6.5 fusion.47
  577.3 7.1 all-to-all-done.3
  592.4 90.4 %all-reduce.10.cloned.1.call-done = (f32[512,512]{1,0:T(8,128)}, f32[512,512]{1,0:T(8,128)}) async-done(((f32[512,512]{1,0:T(8,128)}, f32[512,512]{1,0:T(8,128)}), (f32[512,512]{1,0:T(8,128)}, f32[512,512]{1,0:T(8,128)})) %all-reduce.10.cloned.1.call-update) | async-done | bytes 2097168 | tf_op jit(solution)/shard_map/psum | solution.py:141
  690.3 22.8 %psum.43 = bf16[30,512]{1,0:T(8,128)(2,1)S(1)} all-reduce(bf16[30,512]{1,0:T(8,128)(2,1)S(1)} %bitcast_reduce_fusion.1), channel_id=1, replica_groups=mesh['var'=8,'patch'=8,'win'=2] {'patch'}, use_global_device_ids=true, to_apply=%region_7.8 | all-reduce | flops 15360 | bytes 61440 | tf_op jit(solution)/shard_map/psum | solution.py:139
  713.7 28.8 %all-reduce.6.cloned.1.call-done = bf16[30,16,512]{2,1,0:T(8,128)(2,1)} async-done(((bf16[30,16,512]{2,1,0:T(8,128)(2,1)}), bf16[30,16,512]{2,1,0:T(8,128)(2,1)}) %all-reduce.6.cloned.1.call-update) | async-done | bytes 491536 | tf_op jit(solution)/shard_map/psum | solution.py:138
  744.5 65.8 %all-reduce.8.cloned.1.call-done = (f32[512,512]{1,0:T(8,128)}, f32[512,512]{1,0:T(8,128)}) async-done(((f32[512,512]{1,0:T(8,128)}, f32[512,512]{1,0:T(8,128)}), (f32[512,512]{1,0:T(8,128)}, f32[512,512]{1,0:T(8,128)})) %all-reduce.8.cloned.1.call-update) | async-done | bytes 2097168 | tf_op jit(solution)/shard_map/psum | solution.py:141
  (84 shorter events, 53.6 us)
Async XLA Ops:
  7.2 271.4 %copy-start = (bf16[512,512]{1,0:T(8,128)(2,1)S(1)}, bf16[512,512]{1,0:T(8,128)(2,1)}, u32[]{:S(2)}) copy-start(bf16[512,512]{1,0:T(8,128)(2,1)} %param.21) | copy-start | bytes 1572868
  14.1 11.4 %copy-start.9 = (bf16[30,128,16]{1,2,0:T(8,128)(2,1)}, bf16[30,128,16]{1,2,0:T(8,128)(2,1)S(1)}, u32[]{:S(2)}) copy-start(bf16[30,128,16]{1,2,0:T(8,128)(2,1)S(1)} %copy.92) | copy-start | bytes 368644
  271.6 6.5 copy-start.4
  271.6 6.7 copy-start.11
  271.6 7.0 copy-start.15
  271.6 7.3 copy-start.16
  271.6 7.4 copy-start.1
  271.6 9.3 %copy-start.17 = (f32[38,8]{0,1:T(8,128)S(1)}, f32[38,8]{0,1:T(8,128)}, u32[]{:S(2)}) copy-start(f32[38,8]{0,1:T(8,128)} %param.23) | copy-start | bytes 3652
  271.6 55.4 %all-to-all-start.1 = ((bf16[240,2,4096]{0,1,2:T(2,128)(2,1)}), bf16[240,2,4096]{0,1,2:T(2,128)(2,1)}, u32[]{:S(2)}, u32[]{:S(2)}) async-start(bf16[240,2,4096]{0,1,2:T(2,128)(2,1)} %copy.96), calls=%async_computation.1 | async-start | bytes 8388608 | tf_op jit(solution)/shard_map/all_to_all | solution.py:114
  279.0 63.9 %copy-start.12 = (bf16[16,8,64]{2,1,0:T(8,128)(2,1)}, bf16[16,8,64]{2,1,0:T(8,128)(2,1)S(1)}, u32[]{:S(2)}) copy-start(bf16[16,8,64]{2,1,0:T(8,128)(2,1)S(1)} %reshape.103) | copy-start | bytes 49156
  281.5 131.8 %copy-start.7 = (bf16[16,8,512]{2,0,1:T(8,128)(2,1)}, bf16[16,8,512]{2,0,1:T(8,128)(2,1)S(1)}, u32[]{:S(2)}) copy-start(bf16[16,8,512]{2,0,1:T(8,128)(2,1)S(1)} %fusion.13) | copy-start | bytes 393220
  373.0 6.8 copy-start.14
  379.8 33.5 %copy-start.3 = (bf16[240,8,2,512]{3,0,2,1:T(8,128)(2,1)S(1)}, bf16[240,8,2,512]{3,0,2,1:T(8,128)(2,1)}, u32[]{:S(2)}) copy-start(bf16[240,8,2,512]{3,0,2,1:T(8,128)(2,1)} %copy.128) | copy-start | bytes 11796484
  413.3 1.1 copy-start.5
  460.6 4.7 copy-start.6
  460.6 4.7 copy-start.8
  529.1 55.3 %all-to-all-start.3 = ((bf16[30,16,4096]{2,0,1:T(8,128)(2,1)}), bf16[30,16,4096]{2,0,1:T(8,128)(2,1)}, u32[]{:S(2)}, u32[]{:S(2)}) async-start(bf16[30,16,4096]{2,0,1:T(8,128)(2,1)} %reshape.142), calls=%async_computation.3 | async-start | bytes 8388608 | tf_op jit(solution)/shard_map/all_to_all | solution.py:124
  535.5 147.3 %all-reduce.10.cloned.1.call-start = ((), (), s32[]{:S(2)}) async-start(), calls=%async_computation.6 | async-start | bytes 4194304 | tf_op jit(solution)/shard_map/psum | solution.py:141
  566.3 2.8 copy-start.13
  577.3 13.3 %copy-start.10 = (bf16[30,128,16]{1,2,0:T(8,128)(2,1)S(1)}, bf16[30,128,16]{1,2,0:T(8,128)(2,1)}, u32[]{:S(2)}) copy-start(bf16[30,128,16]{1,2,0:T(8,128)(2,1)} %copy-done.9) | copy-start | bytes 368644
  577.3 165.2 %all-reduce.6.cloned.1.call-start = ((), (), s32[]{:S(2)}) async-start(), calls=%async_computation.4 | async-start | bytes 983040 | tf_op jit(solution)/shard_map/psum | solution.py:138
  588.8 1.9 copy-start.2
  592.1 218.3 %all-reduce.8.cloned.1.call-start = ((), (), s32[]{:S(2)}) async-start(), calls=%async_computation.5 | async-start | bytes 4194304 | tf_op jit(solution)/shard_map/psum | solution.py:141
Sparse Core Ops, SparseCore 0:
  577.4 105.2 all-reduce.9
  685.7 56.7 all-reduce.5
  745.0 65.2 all-reduce.7
